TPU v7x, 32 devices: a whole 2x2x4 slice. The times are simulated.
32 devices in a mesh: set: 1, kb: 32 (over z, y, x, core).
Axes of the slice: x: 2, y: 2, z: 4, core: 2. Of those that a mesh axis runs over, the one named last changes fastest.
Arguments:
- green_momentum_grid: float32 [2, 4, 4096, 512], P('set', None, 'kb'), may hold values from -6 to 6
- pair_table: int32 [8, 2], replicated, may hold values from 0 to 3, as said below
- mirror_map: int32 [3, 16], P('set'), may hold values from 0 to 15, as said below
Outputs:
- chi_out: float32 [2, 8, 4096, 512], P('set', None, 'kb')
Inputs may be any that keep to these rules, and one draw needn't show every extreme that they name: `pair_table`: each of the two columns names every entry number 0 to 3 at least once. Each row d is a reflection: mirror_map[d,x] = (c_d - x) mod 16 for a centre c_d of that row.
All inputs are finite; a program needn't handle non-finite values.
Results may differ from a plain program's by a relative error of at most 0.0003.
Values sent between devices are 32-bit elements; how exact they have to be, the bound alone decides.
A program may use at most 128 MiB of HBM per device.

v0:
```python
import functools

import numpy as np
import ml_dtypes
import jax
import jax.numpy as jnp
from jax import lax
from jax.experimental import pallas as pl
from jax.experimental.pallas import tpu as pltpu
from jax.sharding import PartitionSpec as P

CHUNKS = 2
VMEM = pl.BlockSpec(memory_space=pltpu.VMEM)
SMEM = pl.BlockSpec(memory_space=pltpu.SMEM)
PARAMS = pltpu.CompilerParams(vmem_limit_bytes=48 * 1024 * 1024)


def split_np(table):
    table = table.astype(np.float32)
    high = table.astype(ml_dtypes.bfloat16)
    low = (table - high.astype(np.float32)).astype(ml_dtypes.bfloat16)
    return high, low


def split(x):
    high = x.astype(jnp.bfloat16)
    return high, (x - high.astype(jnp.float32)).astype(jnp.bfloat16)


def mm(a, b, dims):
    return lax.dot_general(a, b, (dims, ((), ())), preferred_element_type=jnp.float32)


def mm3(a, b, dims=((1,), (0,))):
    return mm(a[0], b[0], dims) + mm(a[1], b[0], dims) + mm(a[0], b[1], dims)


def owned_times(devices, freqs, chunk):
    per = freqs // (2 * CHUNKS * devices)
    first = chunk * (freqs // (2 * CHUNKS)) + np.arange(devices)[:, None] * per + np.arange(per)[None, :]
    return np.stack([first, freqs - 1 - first], axis=1).reshape(-1)


def time_tables(times, freqs):
    angle = ((2 * np.arange(freqs)[None, :] - freqs + 1) * (2 * times[:, None] + 1)) % (4 * freqs)
    angle = angle * (2 * np.pi / (4 * freqs))
    scale = freqs**-0.5
    return split_np(scale * np.cos(angle)) + split_np(scale * np.sin(angle))


def frequency_tables(times, freqs):
    angle = ((np.arange(freqs)[None, :] - freqs // 2) * (2 * times[:, None] + 1)) % (2 * freqs)
    angle = angle * (2 * np.pi / (2 * freqs))
    cos, sin = np.cos(angle) * freqs**-0.5, np.sin(angle) * freqs**-0.5
    return split_np(np.block([[cos, sin], [-sin, cos]]))


def plane_table(side, sign):
    index = np.arange(side * side)
    upper, lower = index // side, index % side
    angle = (upper[:, None] * upper[None, :] + lower[:, None] * lower[None, :]) % side * (2 * np.pi / side)
    scale = (side**3) ** -0.5
    cos, sin = scale * np.cos(angle), sign * scale * np.sin(angle)
    return split_np(np.block([[cos, sin], [-sin, cos]]))


def cadd(a, b):
    return a[0] + b[0], a[1] + b[1]


def csub(a, b):
    return a[0] - b[0], a[1] - b[1]


def dft4(a, sign):
    s02, d02 = cadd(a[0], a[2]), csub(a[0], a[2])
    s13, d13 = cadd(a[1], a[3]), csub(a[1], a[3])
    turned = (-d13[1], d13[0]) if sign > 0 else (d13[1], -d13[0])
    return [cadd(s02, s13), cadd(d02, turned), csub(s02, s13), csub(d02, turned)]


def twiddle(a, power, sign):
    if power == 0:
        return a
    if power == 4:
        return (-a[1], a[0]) if sign > 0 else (a[1], -a[0])
    if power in (2, 6):
        r = np.float32(np.sqrt(0.5))
        plus, minus = (a[0] + a[1]) * r, (a[0] - a[1]) * r
        if power == 2:
            return (minus, plus) if sign > 0 else (plus, -minus)
        return (-plus, minus) if sign > 0 else (-minus, -plus)
    c = np.float32(np.cos(2 * np.pi * power / 16))
    s = np.float32(sign * np.sin(2 * np.pi * power / 16))
    return a[0] * c - a[1] * s, a[0] * s + a[1] * c


def dft16(x, sign):
    columns = [dft4([x[4 * n1 + n2] for n1 in range(4)], sign) for n2 in range(4)]
    out = [None] * 16
    for k1 in range(4):
        row = dft4([twiddle(columns[n2][k1], n2 * k1, sign) for n2 in range(4)], sign)
        for k2 in range(4):
            out[k1 + 4 * k2] = row[k2]
    return out


def to_time_kernel(g_ref, ch_ref, cl_ref, sh_ref, sl_ref, o_ref):
    devices, _, entries, slots, points = o_ref.shape
    freqs = g_ref.shape[-1]
    cos, sin = (ch_ref[...], cl_ref[...]), (sh_ref[...], sl_ref[...])
    dims = ((1,), (1,))
    re = split(g_ref[0].reshape(entries * points, freqs))
    im = split(g_ref[1].reshape(entries * points, freqs))
    tau = (mm3(cos, re, dims) + mm3(sin, im, dims), mm3(cos, im, dims) - mm3(sin, re, dims))
    for part in range(2):
        for e in range(entries):
            o_ref[:, part, e] = tau[part][:, e * points:(e + 1) * points].reshape(devices, slots, points)


def bubble_kernel(pair_ref, mirror_ref, x_ref, wh_ref, wl_ref, mh_ref, ml_ref, ih_ref, il_ref, o_ref, y, g, gm, chi):
    devices, _, entries, slots, points = x_ref.shape
    side = y.shape[0]
    plane = side * side
    halves = devices // side
    comps = o_ref.shape[2]
    for h in range(halves):
        for e in range(entries):
            cells = [(x_ref[k * halves + h, 0, e], x_ref[k * halves + h, 1, e]) for k in range(side)]
            for k, (re, im) in enumerate(dft16(cells, 1)):
                y[k, e, :, h * points:(h + 1) * points] = re
                y[k, e, :, plane + h * points:plane + (h + 1) * points] = im
    rows = split(y[...].reshape(side * entries * slots, 2 * plane))
    g[...] = mm3(rows, (wh_ref[...], wl_ref[...])).reshape(g.shape)
    other = mm3(rows, (mh_ref[...], ml_ref[...])).reshape(side * entries, slots, 2 * plane)
    other = jnp.concatenate([other[:, slots // 2:], other[:, :slots // 2]], axis=1)
    gm[...] = other.reshape(gm.shape)

    def one(c, carry):
        left, right = pair_ref[c, 0], pair_ref[c, 1]
        for r in range(side):
            a = g[r, left]
            b = gm[mirror_ref[0, r], right]
            ar, ai, br, bi = a[:, :plane], a[:, plane:], b[:, :plane], b[:, plane:]
            chi[c, r, :, :plane] = ar * br - ai * bi
            chi[c, r, :, plane:] = ar * bi + ai * br
        return carry

    lax.fori_loop(0, comps, one, 0)
    rows = split(chi[...].reshape(comps * side * slots, 2 * plane))
    chi[...] = mm3(rows, (ih_ref[...], il_ref[...])).reshape(chi.shape)

    def back(c, carry):
        for h in range(halves):
            lanes = slice(h * points, (h + 1) * points)
            high = slice(plane + h * points, plane + (h + 1) * points)
            cells = [(chi[c, r, :, lanes], chi[c, r, :, high]) for r in range(side)]
            for q, (re, im) in enumerate(dft16(cells, -1)):
                o_ref[q * halves + h, 0, c] = re
                o_ref[q * halves + h, 1, c] = im
        return carry

    lax.fori_loop(0, comps, back, 0)


def to_frequency_kernel(first, *refs):
    x_ref, bh_ref, bl_ref = refs[:3]
    o_ref = refs[-1]
    devices, _, block, slots, points = x_ref.shape
    freqs = o_ref.shape[-1]
    rows = []
    for c in range(block):
        parts = [x_ref[:, part, c].reshape(devices * slots, points).T for part in range(2)]
        rows.append(jnp.concatenate(parts, axis=1))
    value = mm3(split(jnp.concatenate(rows, axis=0)), (bh_ref[...], bl_ref[...]))
    for part in range(2):
        lanes = value[:, part * freqs:(part + 1) * freqs].reshape(block, points, freqs)
        o_ref[part] = lanes if first else refs[3][part] + lanes


def local(devices, green, pair_table, mirror_map):
    entries, points, freqs = green.shape[1:]
    side = mirror_map.shape[1]
    plane = side * side
    comps = pair_table.shape[0]
    slots = freqs // (devices * CHUNKS)
    f32 = jnp.float32
    ahead = plane_table(side, 1.0)
    inverse = plane_table(side, -1.0)
    target = (mirror_map[1][:, None] * side + mirror_map[2][None, :]).reshape(1, plane)
    pick = (lax.broadcasted_iota(jnp.int32, (plane, plane), 0) == target).astype(jnp.bfloat16)
    mirrored = [
        jnp.einsum("apk,kr->apr", t.reshape(2 * plane, 2, plane), pick, preferred_element_type=jnp.bfloat16)
        .reshape(2 * plane, 2 * plane)
        for t in ahead
    ]
    times = [owned_times(devices, freqs, p) for p in range(CHUNKS)]
    moved = []
    for p in range(CHUNKS):
        tau = pl.pallas_call(
            to_time_kernel,
            out_shape=jax.ShapeDtypeStruct((devices, 2, entries, slots, points), f32),
            in_specs=[VMEM] * 5,
            out_specs=VMEM,
            compiler_params=PARAMS,
            cost_estimate=pl.CostEstimate(flops=6 * 10**9 // CHUNKS, bytes_accessed=8 * 2**20, transcendentals=0),
        )(green, *time_tables(times[p], freqs))
        moved.append(lax.all_to_all(tau, "kb", 0, 0, tiled=True))
    arrived = []
    for p in range(CHUNKS):
        chi = pl.pallas_call(
            bubble_kernel,
            out_shape=jax.ShapeDtypeStruct((devices, 2, comps, slots, points), f32),
            in_specs=[SMEM, SMEM] + [VMEM] * 7,
            out_specs=VMEM,
            scratch_shapes=[
                pltpu.VMEM((side, entries, slots, 2 * plane), f32),
                pltpu.VMEM((side, entries, slots, 2 * plane), f32),
                pltpu.VMEM((side, entries, slots, 2 * plane), f32),
                pltpu.VMEM((comps, side, slots, 2 * plane), f32),
            ],
            compiler_params=PARAMS,
            cost_estimate=pl.CostEstimate(flops=12 * 10**9 // CHUNKS, bytes_accessed=16 * 2**20, transcendentals=0),
        )(pair_table, mirror_map, moved[p], *ahead, *mirrored, *inverse)
        arrived.append(lax.all_to_all(chi, "kb", 0, 0, tiled=True))
    out = None
    block = comps // 2
    for p in range(CHUNKS):
        table = pl.BlockSpec((2 * freqs // CHUNKS, 2 * freqs), lambda i: (0, 0))
        result = pl.BlockSpec((2, block, points, freqs), lambda i: (0, i, 0, 0))
        out = pl.pallas_call(
            functools.partial(to_frequency_kernel, out is None),
            grid=(comps // block,),
            out_shape=jax.ShapeDtypeStruct((2, comps, points, freqs), f32),
            in_specs=[pl.BlockSpec((devices, 2, block, slots, points), lambda i: (0, 0, i, 0, 0)), table, table]
            + ([] if out is None else [result]),
            out_specs=result,
            input_output_aliases={} if out is None else {3: 0},
            compiler_params=PARAMS,
            cost_estimate=pl.CostEstimate(flops=12 * 10**9 // CHUNKS, bytes_accessed=16 * 2**20, transcendentals=0),
        )(arrived[p], *frequency_tables(times[p], freqs), *([] if out is None else [out]))
    return out


def solution(mesh):
    placed = (P("set", None, "kb", None), P(), P("set", None))
    return jax.shard_map(
        functools.partial(local, mesh.shape["kb"]),
        mesh=mesh,
        in_specs=placed,
        out_specs=P("set", None, "kb", None),
        check_vma=False,
    )
```

profile of v0, /device:TPU:0, one launch (start us, length us, event | category | flops | bytes accessed | tf_op | source)
XLA Modules:
  0.0 185.4 jit_solution(3461913660068985758)
XLA Ops:
  0.0 1.6 copy-done.5
  5.4 2.8 %shard_map.201 = f32[32,2,4,8,128]{4,3,2,1,0:T(8,128)} custom-call(f32[2,4,128,512]{3,2,1,0:T(8,128)S(1)} %copy-done.5, bf16[256,512]{1,0:T(8,128)(2,1)S(1)} %copy-done.26, bf16[256,512]{1,0:T(8,128)(2,1)S(1)} %copy-done.25, bf16[256,512]{1,0:T(8,128)(2,1)S(1)} %copy-done.24, bf16[256,512]{1,0:T(8,128)(2,1)S(1)} %copy-done.23), custom_call_target="tpu_custom_call" | custom-call | flops 3000000000 | bytes 8388608 | tf_op jit(solution)/shard_map/pallas_call | solution.py:200
  8.2 7.3 %all-to-all-start.2 = ((f32[32,2,4,8,128]{4,3,2,1,0:T(8,128)}), f32[32,2,4,8,128]{4,3,2,1,0:T(8,128)S(1)}, u32[]{:S(2)}, u32[]{:S(2)}) async-start(f32[32,2,4,8,128]{4,3,2,1,0:T(8,128)} %shard_map.201), calls=%async_computation.2 | async-start | bytes 2097152 | tf_op jit(solution)/shard_map/all_to_all | solution.py:208
  18.4 2.8 %shard_map.199 = f32[32,2,4,8,128]{4,3,2,1,0:T(8,128)} custom-call(f32[2,4,128,512]{3,2,1,0:T(8,128)S(1)} %copy-done.6, bf16[256,512]{1,0:T(8,128)(2,1)S(1)} %copy-done.22, bf16[256,512]{1,0:T(8,128)(2,1)S(1)} %copy-done.21, bf16[256,512]{1,0:T(8,128)(2,1)S(1)} %copy-done.20, bf16[256,512]{1,0:T(8,128)(2,1)S(1)} %copy-done.19), custom_call_target="tpu_custom_call" | custom-call | flops 3000000000 | bytes 8388608 | tf_op jit(solution)/shard_map/pallas_call | solution.py:200
  21.2 20.6 %all-to-all-done.2.x_ref = f32[32,2,4,8,128]{4,3,2,1,0:T(8,128)S(1)} async-done(((f32[32,2,4,8,128]{4,3,2,1,0:T(8,128)}), f32[32,2,4,8,128]{4,3,2,1,0:T(8,128)S(1)}, u32[]{:S(2)}, u32[]{:S(2)}) %all-to-all-start.2) | async-done | bytes 1048608 | tf_op jit(solution)/shard_map/all_to_all | solution.py:208
  41.7 3.6 %all-to-all-start = ((f32[32,2,4,8,128]{4,3,2,1,0:T(8,128)}), f32[32,2,4,8,128]{4,3,2,1,0:T(8,128)S(1)}, u32[]{:S(2)}, u32[]{:S(2)}) async-start(f32[32,2,4,8,128]{4,3,2,1,0:T(8,128)} %shard_map.199), calls=%async_computation | async-start | bytes 2097152 | tf_op jit(solution)/shard_map/all_to_all | solution.py:208
  46.2 2.4 %fusion.3 = bf16[512,2,256]{0,2,1:T(8,128)(2,1)} fusion(bf16[512,2,256]{2,0,1:T(8,128)(2,1)} %constant.38.clone, s32[256]{0:T(256)S(1)} %add.26), kind=kOutput, calls=%fused_computation.3 | convolution fusion | flops 134283264 | bytes 1049600 | tf_op jit(solution)/shard_map/apk,kr->apr/dot_general | solution.py:193
  48.6 1.3 copy.27.mh_ref
  51.9 1.0 copy-done.15
  53.0 1.0 copy-done.17
  54.0 6.6 %shard_map.202 = f32[32,2,8,8,128]{4,3,2,1,0:T(8,128)} custom-call(s32[8,2]{1,0:T(8,128)S(1)} %copy.25.pair_ref, s32[3,16]{1,0:T(4,128)S(1)} %copy-done.4, f32[32,2,4,8,128]{4,3,2,1,0:T(8,128)S(1)} %all-to-all-done.2.x_ref, bf16[512,512]{1,0:T(8,128)(2,1)S(1)} %copy-done.17, bf16[512,512]{1,0:T(8,128)(2,1)S(1)} %copy-done.15, ...), custom_call_target="tpu_custom_call" | custom-call | flops 6000000000 | bytes 16777216 | tf_op jit(solution)/shard_map/pallas_call | solution.py:211
  60.6 11.0 %all-to-all-done.x_ref = f32[32,2,4,8,128]{4,3,2,1,0:T(8,128)S(1)} async-done(((f32[32,2,4,8,128]{4,3,2,1,0:T(8,128)}), f32[32,2,4,8,128]{4,3,2,1,0:T(8,128)S(1)}, u32[]{:S(2)}, u32[]{:S(2)}) %all-to-all-start) | async-done | bytes 1048608 | tf_op jit(solution)/shard_map/all_to_all | solution.py:208
  71.6 3.6 %all-to-all-start.3 = ((f32[32,2,8,8,128]{4,3,2,1,0:T(8,128)}), f32[32,2,8,8,128]{4,3,2,1,0:T(8,128)S(1)}, u32[]{:S(2)}, u32[]{:S(2)}) async-start(f32[32,2,8,8,128]{4,3,2,1,0:T(8,128)} %shard_map.202), calls=%async_computation.3 | async-start | bytes 4194304 | tf_op jit(solution)/shard_map/all_to_all | solution.py:225
  76.3 1.0 copy-done.3
  77.3 1.0 copy-done.12
  81.5 6.6 %shard_map.200 = f32[32,2,8,8,128]{4,3,2,1,0:T(8,128)} custom-call(s32[8,2]{1,0:T(8,128)S(1)} %copy.25.pair_ref, s32[3,16]{1,0:T(4,128)S(1)} %copy-done.4, f32[32,2,4,8,128]{4,3,2,1,0:T(8,128)S(1)} %all-to-all-done.x_ref, bf16[512,512]{1,0:T(8,128)(2,1)S(1)} %copy-done.18, bf16[512,512]{1,0:T(8,128)(2,1)S(1)} %copy-done.16, bf16[512,512]{1,0:T(8,128)(2,1)S(1)} %copy-done.3, ...), custom_call_target="tpu_custom_call" | custom-call | flops 6000000000 | bytes 16777216 | tf_op jit(solution)/shard_map/pallas_call | solution.py:211
  88.1 36.1 %all-to-all-done.3.refs_0_ = f32[32,2,8,8,128]{4,3,2,1,0:T(8,128)S(1)} async-done(((f32[32,2,8,8,128]{4,3,2,1,0:T(8,128)}), f32[32,2,8,8,128]{4,3,2,1,0:T(8,128)S(1)}, u32[]{:S(2)}, u32[]{:S(2)}) %all-to-all-start.3) | async-done | bytes 2097184 | tf_op jit(solution)/shard_map/all_to_all | solution.py:225
  124.1 4.3 %all-to-all-start.1 = ((f32[32,2,8,8,128]{4,3,2,1,0:T(8,128)}), f32[32,2,8,8,128]{4,3,2,1,0:T(8,128)}, u32[]{:S(2)}, u32[]{:S(2)}) async-start(f32[32,2,8,8,128]{4,3,2,1,0:T(8,128)} %shard_map.200), calls=%async_computation.1 | async-start | bytes 4194304 | tf_op jit(solution)/shard_map/all_to_all | solution.py:225
  128.5 1.2 copy-done.9
  129.7 1.2 copy-done.10
  130.9 5.2 %shard_map.203.refs_3_ = f32[2,8,128,512]{3,2,1,0:T(8,128)} custom-call(f32[32,2,8,8,128]{4,3,2,1,0:T(8,128)S(1)} %all-to-all-done.3.refs_0_, bf16[512,1024]{1,0:T(8,128)(2,1)S(1)} %copy-done.10, bf16[512,1024]{1,0:T(8,128)(2,1)S(1)} %copy-done.9), custom_call_target="tpu_custom_call" | custom-call | flops 6000000000 | bytes 16777216 | tf_op jit(solution)/shard_map/pallas_call | solution.py:231
  136.1 41.1 %all-to-all-done.1.refs_0_ = f32[32,2,8,8,128]{4,3,2,1,0:T(8,128)} async-done(((f32[32,2,8,8,128]{4,3,2,1,0:T(8,128)}), f32[32,2,8,8,128]{4,3,2,1,0:T(8,128)}, u32[]{:S(2)}, u32[]{:S(2)}) %all-to-all-start.1) | async-done | bytes 2097184 | tf_op jit(solution)/shard_map/all_to_all | solution.py:225
  177.2 1.2 copy-done.8
  178.4 6.9 %shard_map.204 = f32[2,8,128,512]{3,2,1,0:T(8,128)} custom-call(f32[32,2,8,8,128]{4,3,2,1,0:T(8,128)} %all-to-all-done.1.refs_0_, bf16[512,1024]{1,0:T(8,128)(2,1)S(1)} %copy-done.8, bf16[512,1024]{1,0:T(8,128)(2,1)S(1)} %copy-done.7, f32[2,8,128,512]{3,2,1,0:T(8,128)} %shard_map.203.refs_3_), custom_call_target="tpu_custom_call", output_to_operand_aliasing={{}: (3, {})} | custom-call | flops 6000000000 | bytes 16777216 | tf_op jit(solution)/shard_map/pallas_call | solution.py:231
  (56 shorter events, 13.7 us)
Async XLA Ops:
  0.0 1.6 copy-start.5
  5.4 10.1 %copy-start.6 = (f32[2,4,128,512]{3,2,1,0:T(8,128)S(1)}, f32[2,4,128,512]{3,2,1,0:T(8,128)}, u32[]{:S(2)}) copy-start(f32[2,4,128,512]{3,2,1,0:T(8,128)} %g_ref.3) | copy-start | bytes 6291460
  5.4 10.1 %copy-start.19 = (bf16[256,512]{1,0:T(8,128)(2,1)S(1)}, bf16[256,512]{1,0:T(8,128)(2,1)}, u32[]{:S(2)}) copy-start(bf16[256,512]{1,0:T(8,128)(2,1)} %constant.47.clone.sl_ref) | copy-start | bytes 786436
  8.2 33.5 %all-to-all-start.2 = ((f32[32,2,4,8,128]{4,3,2,1,0:T(8,128)}), f32[32,2,4,8,128]{4,3,2,1,0:T(8,128)S(1)}, u32[]{:S(2)}, u32[]{:S(2)}) async-start(f32[32,2,4,8,128]{4,3,2,1,0:T(8,128)} %shard_map.201), calls=%async_computation.2 | async-start | bytes 2097152 | tf_op jit(solution)/shard_map/all_to_all | solution.py:208
  21.2 24.2 %copy-start.28 = (s32[8,2]{0,1:T(2,128)S(1)}, s32[8,2]{0,1:T(2,128)}, u32[]{:S(2)}) copy-start(s32[8,2]{0,1:T(2,128)} %param.22) | copy-start | bytes 196
  21.2 24.3 %copy-start.4 = (s32[3,16]{1,0:T(4,128)S(1)}, s32[3,16]{1,0:T(4,128)}, u32[]{:S(2)}) copy-start(s32[3,16]{1,0:T(4,128)} %mirror_ref.3) | copy-start | bytes 580
  21.2 24.5 %copy-start.27 = (bf16[512,2,256]{2,0,1:T(8,128)(2,1)S(1)}, bf16[512,2,256]{2,0,1:T(8,128)(2,1)}, u32[]{:S(2)}) copy-start(bf16[512,2,256]{2,0,1:T(8,128)(2,1)} %constant.39.clone) | copy-start | bytes 1572868
  41.7 29.9 %all-to-all-start = ((f32[32,2,4,8,128]{4,3,2,1,0:T(8,128)}), f32[32,2,4,8,128]{4,3,2,1,0:T(8,128)S(1)}, u32[]{:S(2)}, u32[]{:S(2)}) async-start(f32[32,2,4,8,128]{4,3,2,1,0:T(8,128)} %shard_map.199), calls=%async_computation | async-start | bytes 2097152 | tf_op jit(solution)/shard_map/all_to_all | solution.py:208
  46.2 14.4 %copy-start = (bf16[512,512]{1,0:T(8,128)(2,1)}, bf16[512,512]{1,0:T(8,128)(2,1)S(1)}, u32[]{:S(2)}) copy-start(bf16[512,512]{1,0:T(8,128)(2,1)S(1)} %copy.28.ml_ref) | copy-start | bytes 1572868
  49.8 1.0 copy-start.11
  50.9 1.0 copy-start.13
  51.9 1.0 copy-start.15
  53.0 1.0 copy-start.17
  54.0 6.6 %copy-start.2 = (bf16[512,512]{1,0:T(8,128)(2,1)}, bf16[512,512]{1,0:T(8,128)(2,1)S(1)}, u32[]{:S(2)}) copy-start(bf16[512,512]{1,0:T(8,128)(2,1)S(1)} %copy.27.mh_ref) | copy-start | bytes 1572868
  71.6 52.5 %all-to-all-start.3 = ((f32[32,2,8,8,128]{4,3,2,1,0:T(8,128)}), f32[32,2,8,8,128]{4,3,2,1,0:T(8,128)S(1)}, u32[]{:S(2)}, u32[]{:S(2)}) async-start(f32[32,2,8,8,128]{4,3,2,1,0:T(8,128)} %shard_map.202), calls=%async_computation.3 | async-start | bytes 4194304 | tf_op jit(solution)/shard_map/all_to_all | solution.py:225
  75.2 1.0 copy-start.1
  76.3 1.0 copy-start.3
  77.3 1.0 copy-start.12
  78.4 1.0 copy-start.14
  124.1 53.1 %all-to-all-start.1 = ((f32[32,2,8,8,128]{4,3,2,1,0:T(8,128)}), f32[32,2,8,8,128]{4,3,2,1,0:T(8,128)}, u32[]{:S(2)}, u32[]{:S(2)}) async-start(f32[32,2,8,8,128]{4,3,2,1,0:T(8,128)} %shard_map.200), calls=%async_computation.1 | async-start | bytes 4194304 | tf_op jit(solution)/shard_map/all_to_all | solution.py:225
  128.5 1.2 copy-start.9
  129.7 1.2 copy-start.10
  130.9 46.3 %copy-start.7 = (bf16[512,1024]{1,0:T(8,128)(2,1)S(1)}, bf16[512,1024]{1,0:T(8,128)(2,1)}, u32[]{:S(2)}) copy-start(bf16[512,1024]{1,0:T(8,128)(2,1)} %constant.55.clone.refs_2_) | copy-start | bytes 3145732
  177.2 1.2 copy-start.8
  (9 other events, 8.7 us)
where the time goes:
time: 187 us; the launch traced here: 185 us
  waiting for transfers between devices  109 us (58%)
  Pallas kernels  30.8 us (16%)
  local copies, waits for them, and re-layouts  24 us (13%)
  starting transfers between devices  18.9 us (10%)
  matrix products  2.73 us (1%)
    all_to_all x2, waiting for transfers between devices, local(): arrived.append(lax.all_to_all(chi, 'kb', 0, 0, tiled=True))  77.2 us
    all_to_all x2, waiting for transfers between devices, local(): moved.append(lax.all_to_all(tau, 'kb', 0, 0, tiled=True))  31.6 us
    unnamed x59, local copies, waits for them, and re-layouts  22.4 us
    pallas_call x2, Pallas kernels, local(): pl.pallas_call(bubble_kernel, out_shape=jax.ShapeDtypeStruct((devices, 2,...  13.1 us
    pallas_call x2, Pallas kernels, local(): pl.pallas_call(functools.partial(to_frequency_kernel, out is None), grid=...  12.1 us
    all_to_all x2, starting transfers between devices, local(): moved.append(lax.all_to_all(tau, 'kb', 0, 0, tiled=True))  10.9 us
    all_to_all x2, starting transfers between devices, local(): arrived.append(lax.all_to_all(chi, 'kb', 0, 0, tiled=True))  7.94 us
    pallas_call x2, Pallas kernels, local(): pl.pallas_call(to_time_kernel, out_shape=jax.ShapeDtypeStruct((devices, 2...  5.59 us
  transfers between devices with their start and end apart: 4, of which 4 were waited for; matrix products, arithmetic and copies ran while one was open for 2% of the time, Pallas kernels for 11%

commit v1 on v0

v1 whole, which is shorter than its diff:
```python
import functools

import numpy as np
import ml_dtypes
import jax
import jax.numpy as jnp
from jax import lax
from jax.experimental import pallas as pl
from jax.experimental.pallas import tpu as pltpu
from jax.sharding import PartitionSpec as P

CHUNKS = 2
VMEM = pl.BlockSpec(memory_space=pltpu.VMEM)
SMEM = pl.BlockSpec(memory_space=pltpu.SMEM)
PARAMS = pltpu.CompilerParams(vmem_limit_bytes=48 * 1024 * 1024)


def split_np(table):
    table = table.astype(np.float32)
    high = table.astype(ml_dtypes.bfloat16)
    low = (table - high.astype(np.float32)).astype(ml_dtypes.bfloat16)
    return high, low


def split(x):
    high = x.astype(jnp.bfloat16)
    return high, (x - high.astype(jnp.float32)).astype(jnp.bfloat16)


def mm(a, b, dims):
    return lax.dot_general(a, b, (dims, ((), ())), preferred_element_type=jnp.float32)


def mm3(a, b, dims=((1,), (0,))):
    return mm(a[0], b[0], dims) + mm(a[1], b[0], dims) + mm(a[0], b[1], dims)


def owned_times(devices, freqs, chunk):
    per = freqs // (2 * CHUNKS * devices)
    first = chunk * (freqs // (2 * CHUNKS)) + np.arange(devices)[:, None] * per + np.arange(per)[None, :]
    return np.stack([first, freqs - 1 - first], axis=1).reshape(-1)


def time_tables(times, freqs):
    angle = ((2 * np.arange(freqs)[None, :] - freqs + 1) * (2 * times[:, None] + 1)) % (4 * freqs)
    angle = angle * (2 * np.pi / (4 * freqs))
    scale = freqs**-0.5
    return split_np(scale * np.cos(angle)) + split_np(scale * np.sin(angle))


def frequency_tables(times, freqs):
    angle = ((np.arange(freqs)[None, :] - freqs // 2) * (2 * times[:, None] + 1)) % (2 * freqs)
    angle = angle * (2 * np.pi / (2 * freqs))
    cos, sin = np.cos(angle) * freqs**-0.5, np.sin(angle) * freqs**-0.5
    return split_np(np.block([[cos, sin], [-sin, cos]]))


def plane_table(side, sign):
    index = np.arange(side * side)
    upper, lower = index // side, index % side
    angle = (upper[:, None] * upper[None, :] + lower[:, None] * lower[None, :]) % side * (2 * np.pi / side)
    scale = (side**3) ** -0.5
    cos, sin = scale * np.cos(angle), sign * scale * np.sin(angle)
    return split_np(np.block([[cos, sin], [-sin, cos]]))


def cadd(a, b):
    return a[0] + b[0], a[1] + b[1]


def csub(a, b):
    return a[0] - b[0], a[1] - b[1]


def dft4(a, sign):
    s02, d02 = cadd(a[0], a[2]), csub(a[0], a[2])
    s13, d13 = cadd(a[1], a[3]), csub(a[1], a[3])
    turned = (-d13[1], d13[0]) if sign > 0 else (d13[1], -d13[0])
    return [cadd(s02, s13), cadd(d02, turned), csub(s02, s13), csub(d02, turned)]


def twiddle(a, power, sign):
    if power == 0:
        return a
    if power == 4:
        return (-a[1], a[0]) if sign > 0 else (a[1], -a[0])
    if power in (2, 6):
        r = np.float32(np.sqrt(0.5))
        plus, minus = (a[0] + a[1]) * r, (a[0] - a[1]) * r
        if power == 2:
            return (minus, plus) if sign > 0 else (plus, -minus)
        return (-plus, minus) if sign > 0 else (-minus, -plus)
    c = np.float32(np.cos(2 * np.pi * power / 16))
    s = np.float32(sign * np.sin(2 * np.pi * power / 16))
    return a[0] * c - a[1] * s, a[0] * s + a[1] * c


def dft16(x, sign):
    columns = [dft4([x[4 * n1 + n2] for n1 in range(4)], sign) for n2 in range(4)]
    out = [None] * 16
    for k1 in range(4):
        row = dft4([twiddle(columns[n2][k1], n2 * k1, sign) for n2 in range(4)], sign)
        for k2 in range(4):
            out[k1 + 4 * k2] = row[k2]
    return out


def to_time(g_ref, table, o_ref, p):
    devices, _, entries, slots, points = o_ref.shape[1:]
    freqs = g_ref.shape[-1]
    cos, sin = (table[p, 0], table[p, 1]), (table[p, 2], table[p, 3])
    dims = ((1,), (1,))
    re = split(g_ref[0].reshape(entries * points, freqs))
    im = split(g_ref[1].reshape(entries * points, freqs))
    tau = (mm3(cos, re, dims) + mm3(sin, im, dims), mm3(cos, im, dims) - mm3(sin, re, dims))
    for part in range(2):
        for e in range(entries):
            o_ref[p, :, part, e] = tau[part][:, e * points:(e + 1) * points].reshape(devices, slots, points)


def bubble(pair_ref, mirror_ref, x_ref, ahead, mirrored, inverse, o_ref, y, g, gm, chi, p):
    devices, _, entries, slots, points = x_ref.shape[1:]
    side = y.shape[0]
    plane = side * side
    halves = devices // side
    comps = o_ref.shape[3]

    def forth(e, carry):
        for h in range(halves):
            cells = [(x_ref[p, k * halves + h, 0, e], x_ref[p, k * halves + h, 1, e]) for k in range(side)]
            for k, (re, im) in enumerate(dft16(cells, 1)):
                y[k, e, :, h * points:(h + 1) * points] = re
                y[k, e, :, plane + h * points:plane + (h + 1) * points] = im
        return carry

    lax.fori_loop(0, entries, forth, 0)
    rows = split(y[...].reshape(side * entries * slots, 2 * plane))
    g[...] = mm3(rows, (ahead[0], ahead[1])).reshape(g.shape)
    other = mm3(rows, (mirrored[0], mirrored[1])).reshape(side * entries, slots, 2 * plane)
    other = jnp.concatenate([other[:, slots // 2:], other[:, :slots // 2]], axis=1)
    gm[...] = other.reshape(gm.shape)

    def one(c, carry):
        left, right = pair_ref[c, 0], pair_ref[c, 1]
        for r in range(side):
            a = g[r, left]
            b = gm[mirror_ref[0, r], right]
            ar, ai, br, bi = a[:, :plane], a[:, plane:], b[:, :plane], b[:, plane:]
            chi[c, r, :, :plane] = ar * br - ai * bi
            chi[c, r, :, plane:] = ar * bi + ai * br
        return carry

    lax.fori_loop(0, comps, one, 0)
    rows = split(chi[...].reshape(comps * side * slots, 2 * plane))
    chi[...] = mm3(rows, (inverse[0], inverse[1])).reshape(chi.shape)

    def back(c, carry):
        for h in range(halves):
            lanes = slice(h * points, (h + 1) * points)
            high = slice(plane + h * points, plane + (h + 1) * points)
            cells = [(chi[c, r, :, lanes], chi[c, r, :, high]) for r in range(side)]
            for q, (re, im) in enumerate(dft16(cells, -1)):
                o_ref[p, q * halves + h, 0, c] = re
                o_ref[p, q * halves + h, 1, c] = im
        return carry

    lax.fori_loop(0, comps, back, 0)


def main_kernel(pair_ref, mirror_ref, g_hbm, time_hbm, plane_hbm, o_hbm,
                green, table, planes, mirrored, tau, x, y, g, gm, chi, sent,
                load, own, send, recv):
    devices = tau.shape[1]
    side = y.shape[0]
    plane = side * side
    me = lax.axis_index("kb")
    loads = [pltpu.make_async_copy(src, dst, load.at[i])
             for i, (src, dst) in enumerate([(g_hbm, green), (time_hbm, table), (plane_hbm, planes)])]
    for copy in loads:
        copy.start()
    barrier = pltpu.get_barrier_semaphore()

    def greet(s, carry):
        pl.semaphore_signal(barrier, inc=1, device_id={"kb": lax.rem(me + s, devices)},
                            device_id_type=pl.DeviceIdType.MESH)
        return carry

    lax.fori_loop(1, devices, greet, 0)

    def exchange(src, dst, p, n):
        pltpu.make_async_copy(src.at[p, me], dst.at[p, me], own.at[n]).start()

        def one(i, carry):
            step = (i + 1) // 2
            shift = devices // 2 + step * (2 * lax.rem(i, 2) - 1)
            pltpu.make_async_remote_copy(
                src_ref=src.at[p, me_plus(shift)], dst_ref=dst.at[p, me],
                send_sem=send.at[n], recv_sem=recv.at[n],
                device_id={"kb": me_plus(shift)}, device_id_type=pl.DeviceIdType.MESH,
            ).start()
            return carry

        lax.fori_loop(0, devices - 1, one, 0)

    def me_plus(shift):
        return lax.rem(me + shift, devices)

    def finish(ref, p, sem):
        part = ref.at[p, pl.ds(0, devices - 1)]
        pltpu.make_async_copy(part, part, sem).wait()

    loads[0].wait()
    loads[1].wait()
    for p in range(CHUNKS):
        to_time(green, table, tau, p)
        if p == 0:
            pl.semaphore_wait(barrier, devices - 1)
        exchange(tau, x, p, p)
    loads[2].wait()
    lane = lax.broadcasted_iota(jnp.int32, (plane, plane), 1)
    ry, rz = lane // side, lane % side
    target = (mirror_ref[1, 0] + side - ry) % side * side + (mirror_ref[2, 0] + side - rz) % side
    pick = (lax.broadcasted_iota(jnp.int32, (plane, plane), 0) == target).astype(jnp.float32).astype(jnp.bfloat16)
    for i in range(2):
        for part in range(2):
            lanes = slice(part * plane, (part + 1) * plane)
            mirrored[i, :, lanes] = mm(planes[i, :, lanes], pick, ((1,), (0,))).astype(jnp.bfloat16)
    for p in range(CHUNKS):
        n = CHUNKS + p
        pltpu.make_async_copy(tau.at[p, me], x.at[p, me], own.at[p]).wait()
        finish(x, p, recv.at[p])
        bubble(pair_ref, mirror_ref, x, planes.at[0:2], mirrored, planes.at[2:4], sent, y, g, gm, chi, p)
        exchange(sent, o_hbm, p, n)
    for p in range(CHUNKS):
        n = CHUNKS + p
        finish(tau, p, send.at[p])
        pltpu.make_async_copy(sent.at[p, me], o_hbm.at[p, me], own.at[n]).wait()
        finish(sent, p, send.at[n])
        finish(o_hbm, p, recv.at[n])


def to_frequency_kernel(x_ref, b_ref, o_ref):
    _, devices, _, block, slots, points = x_ref.shape
    freqs = o_ref.shape[-1]
    rows = []
    for c in range(block):
        parts = [x_ref[p, :, part, c].reshape(devices * slots, points).T
                 for p in range(CHUNKS) for part in range(2)]
        rows.append(jnp.concatenate(parts, axis=1))
    value = mm3(split(jnp.concatenate(rows, axis=0)), (b_ref[0], b_ref[1]))
    for part in range(2):
        o_ref[part] = value[:, part * freqs:(part + 1) * freqs].reshape(block, points, freqs)


def local(devices, green, pair_table, mirror_map):
    entries, points, freqs = green.shape[1:]
    side = mirror_map.shape[1]
    plane = side * side
    comps = pair_table.shape[0]
    slots = freqs // (devices * CHUNKS)
    f32, bf16 = jnp.float32, jnp.bfloat16
    times = [owned_times(devices, freqs, p) for p in range(CHUNKS)]
    time_table = np.stack([np.stack(time_tables(t, freqs)) for t in times])
    plane_tables = np.stack(plane_table(side, 1.0) + plane_table(side, -1.0))
    back = [frequency_tables(t, freqs) for t in times]
    frequency_table = np.stack([np.concatenate([b[i] for b in back], axis=0) for i in range(2)])
    hbm = pl.BlockSpec(memory_space=pl.ANY)
    cells = (side, entries, slots, 2 * plane)
    arrived = pl.pallas_call(
        main_kernel,
        out_shape=jax.ShapeDtypeStruct((CHUNKS, devices, 2, comps, slots, points), f32),
        in_specs=[SMEM, SMEM, hbm, hbm, hbm],
        out_specs=hbm,
        scratch_shapes=[
            pltpu.VMEM(green.shape, f32),
            pltpu.VMEM(time_table.shape, bf16),
            pltpu.VMEM(plane_tables.shape, bf16),
            pltpu.VMEM((2, 2 * plane, 2 * plane), bf16),
            pltpu.VMEM((CHUNKS, devices, 2, entries, slots, points), f32),
            pltpu.VMEM((CHUNKS, devices, 2, entries, slots, points), f32),
            pltpu.VMEM(cells, f32),
            pltpu.VMEM(cells, f32),
            pltpu.VMEM(cells, f32),
            pltpu.VMEM((comps,) + (side, slots, 2 * plane), f32),
            pltpu.VMEM((CHUNKS, devices, 2, comps, slots, points), f32),
            pltpu.SemaphoreType.DMA((3,)),
            pltpu.SemaphoreType.DMA((2 * CHUNKS,)),
            pltpu.SemaphoreType.DMA((2 * CHUNKS,)),
            pltpu.SemaphoreType.DMA((2 * CHUNKS,)),
        ],
        compiler_params=pltpu.CompilerParams(
            vmem_limit_bytes=56 * 1024 * 1024, collective_id=0, has_side_effects=True
        ),
        cost_estimate=pl.CostEstimate(flops=18 * 10**9, bytes_accessed=16 * 2**20, transcendentals=0),
    )(pair_table, mirror_map, green, time_table, plane_tables)
    block = comps // 2
    return pl.pallas_call(
        to_frequency_kernel,
        grid=(comps // block,),
        out_shape=jax.ShapeDtypeStruct((2, comps, points, freqs), f32),
        in_specs=[
            pl.BlockSpec((CHUNKS, devices, 2, block, slots, points), lambda i: (0, 0, 0, i, 0, 0)),
            pl.BlockSpec((2, 2 * freqs, 2 * freqs), lambda i: (0, 0, 0)),
        ],
        out_specs=pl.BlockSpec((2, block, points, freqs), lambda i: (0, i, 0, 0)),
        compiler_params=PARAMS,
        cost_estimate=pl.CostEstimate(flops=12 * 10**9, bytes_accessed=16 * 2**20, transcendentals=0),
    )(arrived, frequency_table)


def solution(mesh):
    placed = (P("set", None, "kb", None), P(), P("set", None))
    return jax.shard_map(
        functools.partial(local, mesh.shape["kb"]),
        mesh=mesh,
        in_specs=placed,
        out_specs=P("set", None, "kb", None),
        check_vma=False,
    )
```

time: 187 us -> 160 us (0.86)
  Pallas kernels: 30.8 us -> 155 us
  waiting for transfers between devices: 109 us -> 0 us
  local copies, waits for them, and re-layouts: 24 us -> 3.53 us
  starting transfers between devices: 18.9 us -> 0 us
  matrix products: 2.73 us -> 0 us
    pallas_call x6 -> x2, Pallas kernels: 30.8 us -> 155 us  [the longest x1 145 us: local(): pl.pallas_call(main_kernel, out_shape=jax.ShapeDtypeStruct((CHUNKS, devic...]
    all_to_all x4 -> x0, waiting for transfers between devices: 109 us -> none  [the longest x2 77.2 us: local(): arrived.append(lax.all_to_all(chi, 'kb', 0, 0, tiled=True))]
    unnamed x59 -> x3, local copies, waits for them, and re-layouts: 22.4 us -> 3.53 us
    all_to_all x4 -> x0, starting transfers between devices: 18.9 us -> none  [the longest x2 10.9 us: local(): moved.append(lax.all_to_all(tau, 'kb', 0, 0, tiled=True))]
    dot_general x2 -> x0, matrix products: 2.73 us -> none  [local(): jnp.einsum('apk,kr->apr', t.reshape(2 * plane, 2, plane), pick, preferred...]
  transfers between devices with their start and end apart: 4 -> 0, of which waited for: 4 -> 0; matrix products, arithmetic and copies ran while one was open for 2% -> 0% of each run, Pallas kernels for 11% -> 0%
where the time goes in v1:
time: 160 us; the launch traced here: 159 us
  Pallas kernels  155 us (97%)
  local copies, waits for them, and re-layouts  3.53 us (2%)
    pallas_call x1, Pallas kernels, local(): pl.pallas_call(main_kernel, out_shape=jax.ShapeDtypeStruct((CHUNKS, devic...  145 us
    pallas_call x1, Pallas kernels, local(): pl.pallas_call(to_frequency_kernel, grid=(comps // block,), out_shape=jax...  10.6 us
    unnamed x3, local copies, waits for them, and re-layouts  3.53 us

profile of v1, /device:TPU:0, one launch (start us, length us, event | category | flops | bytes accessed | tf_op | source)
XLA Modules:
  0.0 159.0 jit_solution(6552037323895687714)
XLA Ops:
  0.0 1.3 copy.7.pair_ref
  1.3 144.9 %shard_map.64.x_ref = f32[2,32,2,8,8,128]{5,4,3,2,1,0:T(8,128)} custom-call(s32[8,2]{1,0:T(8,128)} %copy.7.pair_ref, s32[3,16]{1,0:T(4,128)} %mirror_ref.1, f32[2,4,128,512]{3,2,1,0:T(8,128)} %g_hbm.1, bf16[2,4,256,512]{3,2,1,0:T(8,128)(2,1)} %constant.6.clone.time_hbm, bf16[4,512,512]{2,1,0:T(8,128)(2,1)} %constant.7.clone.plane_hbm), custom_call_target="tpu_custom_call" | custom-call | flops 17999998976 | bytes 16777216 | tf_op jit(solution)/shard_map/pallas_call | solution.py:269
  146.3 0.0 copy-start
  146.3 2.2 %copy-done = f32[2,32,2,8,8,128]{5,4,3,2,1,0:T(8,128)S(1)} copy-done((f32[2,32,2,8,8,128]{5,4,3,2,1,0:T(8,128)S(1)}, f32[2,32,2,8,8,128]{5,4,3,2,1,0:T(8,128)}, u32[]{:S(2)}) %copy-start) | copy-done | bytes 4194328
  148.4 10.6 %shard_map.65 = f32[2,8,128,512]{3,2,1,0:T(8,128)} custom-call(f32[2,32,2,8,8,128]{5,4,3,2,1,0:T(8,128)S(1)} %copy-done, bf16[2,1024,1024]{2,1,0:T(8,128)(2,1)} %constant.8.clone.b_ref), custom_call_target="tpu_custom_call" | custom-call | flops 12000000000 | bytes 16777216 | tf_op jit(solution)/shard_map/pallas_call | solution.py:297
Async XLA Ops:
  146.3 2.2 %copy-start = (f32[2,32,2,8,8,128]{5,4,3,2,1,0:T(8,128)S(1)}, f32[2,32,2,8,8,128]{5,4,3,2,1,0:T(8,128)}, u32[]{:S(2)}) copy-start(f32[2,32,2,8,8,128]{5,4,3,2,1,0:T(8,128)} %shard_map.64.x_ref) | copy-start | bytes 12582916

commit v2 on v1

--- a/solution.py
+++ b/solution.py
@@ -10,9 +10,7 @@
 from jax.sharding import PartitionSpec as P
 
 CHUNKS = 2
-VMEM = pl.BlockSpec(memory_space=pltpu.VMEM)
 SMEM = pl.BlockSpec(memory_space=pltpu.SMEM)
-PARAMS = pltpu.CompilerParams(vmem_limit_bytes=48 * 1024 * 1024)
 
 
 def split_np(table):
@@ -141,7 +139,7 @@
     gm[...] = other.reshape(gm.shape)
 
     def one(c, carry):
-        left, right = pair_ref[c, 0], pair_ref[c, 1]
+        left, right = pair_ref[0, c], pair_ref[1, c]
         for r in range(side):
             a = g[r, left]
             b = gm[mirror_ref[0, r], right]
@@ -167,15 +165,15 @@
     lax.fori_loop(0, comps, back, 0)
 
 
-def main_kernel(pair_ref, mirror_ref, g_hbm, time_hbm, plane_hbm, o_hbm,
-                green, table, planes, mirrored, tau, x, y, g, gm, chi, sent,
+def main_kernel(pair_ref, mirror_ref, green, time_hbm, plane_hbm, back_hbm, half_hbm, last,
+                table, planes, back, mirrored, tau, x, y, g, gm, chi, sent, got, acc,
                 load, own, send, recv):
     devices = tau.shape[1]
     side = y.shape[0]
     plane = side * side
     me = lax.axis_index("kb")
     loads = [pltpu.make_async_copy(src, dst, load.at[i])
-             for i, (src, dst) in enumerate([(g_hbm, green), (time_hbm, table), (plane_hbm, planes)])]
+             for i, (src, dst) in enumerate([(time_hbm, table), (plane_hbm, planes), (back_hbm, back)])]
     for copy in loads:
         copy.start()
     barrier = pltpu.get_barrier_semaphore()
@@ -187,36 +185,38 @@
 
     lax.fori_loop(1, devices, greet, 0)
 
-    def exchange(src, dst, p, n):
-        pltpu.make_async_copy(src.at[p, me], dst.at[p, me], own.at[n]).start()
+    def partner(shift):
+        total, bit = 0, 1
+        while bit < devices:
+            total += bit * lax.rem(me // bit + shift // bit, 2)
+            bit *= 2
+        return total
+
+    def exchange(src, dst, n):
+        pltpu.make_async_copy(src.at[me], dst.at[me], own.at[n]).start()
 
         def one(i, carry):
-            step = (i + 1) // 2
-            shift = devices // 2 + step * (2 * lax.rem(i, 2) - 1)
+            other = partner(i // 4 + devices // 4 * lax.rem(i + 2, 4))
             pltpu.make_async_remote_copy(
-                src_ref=src.at[p, me_plus(shift)], dst_ref=dst.at[p, me],
-                send_sem=send.at[n], recv_sem=recv.at[n],
-                device_id={"kb": me_plus(shift)}, device_id_type=pl.DeviceIdType.MESH,
+                src_ref=src.at[other], dst_ref=dst.at[me], send_sem=send.at[n], recv_sem=recv.at[n],
+                device_id={"kb": other}, device_id_type=pl.DeviceIdType.MESH,
             ).start()
             return carry
 
-        lax.fori_loop(0, devices - 1, one, 0)
-
-    def me_plus(shift):
-        return lax.rem(me + shift, devices)
-
-    def finish(ref, p, sem):
-        part = ref.at[p, pl.ds(0, devices - 1)]
+        lax.fori_loop(0, 2, one, 0)
+        lax.fori_loop(3, devices, one, 0)
+
+    def finish(ref, sem):
+        part = ref.at[pl.ds(0, devices - 1)]
         pltpu.make_async_copy(part, part, sem).wait()
 
     loads[0].wait()
-    loads[1].wait()
     for p in range(CHUNKS):
         to_time(green, table, tau, p)
         if p == 0:
             pl.semaphore_wait(barrier, devices - 1)
-        exchange(tau, x, p, p)
-    loads[2].wait()
+        exchange(tau.at[p], x.at[p], p)
+    loads[1].wait()
     lane = lax.broadcasted_iota(jnp.int32, (plane, plane), 1)
     ry, rz = lane // side, lane % side
     target = (mirror_ref[1, 0] + side - ry) % side * side + (mirror_ref[2, 0] + side - rz) % side
@@ -225,31 +225,47 @@
         for part in range(2):
             lanes = slice(part * plane, (part + 1) * plane)
             mirrored[i, :, lanes] = mm(planes[i, :, lanes], pick, ((1,), (0,))).astype(jnp.bfloat16)
+    landing = [got, last]
     for p in range(CHUNKS):
-        n = CHUNKS + p
         pltpu.make_async_copy(tau.at[p, me], x.at[p, me], own.at[p]).wait()
-        finish(x, p, recv.at[p])
+        finish(x.at[p], recv.at[p])
         bubble(pair_ref, mirror_ref, x, planes.at[0:2], mirrored, planes.at[2:4], sent, y, g, gm, chi, p)
-        exchange(sent, o_hbm, p, n)
+        exchange(sent.at[p], landing[p], CHUNKS + p)
+    pltpu.make_async_copy(sent.at[0, me], got.at[me], own.at[CHUNKS]).wait()
+    finish(got, recv.at[CHUNKS])
+    loads[2].wait()
+    comps = got.shape[2]
+    block = comps // 2
+    for i in range(2):
+        chosen = slice(i * block, (i + 1) * block)
+        value = to_frequency(got.at[:, :, chosen], back)
+        for part in range(2):
+            acc[part, chosen] = value[part]
+    store = pltpu.make_async_copy(acc, half_hbm, load.at[3])
+    store.start()
     for p in range(CHUNKS):
-        n = CHUNKS + p
-        finish(tau, p, send.at[p])
-        pltpu.make_async_copy(sent.at[p, me], o_hbm.at[p, me], own.at[n]).wait()
-        finish(sent, p, send.at[n])
-        finish(o_hbm, p, recv.at[n])
-
-
-def to_frequency_kernel(x_ref, b_ref, o_ref):
-    _, devices, _, block, slots, points = x_ref.shape
-    freqs = o_ref.shape[-1]
+        finish(tau.at[p], send.at[p])
+        finish(sent.at[p], send.at[CHUNKS + p])
+    store.wait()
+    pltpu.make_async_copy(sent.at[1, me], last.at[me], own.at[CHUNKS + 1]).wait()
+    finish(last, recv.at[CHUNKS + 1])
+
+
+def to_frequency(x_ref, b_ref):
+    devices, _, block, slots, points = x_ref.shape
+    freqs = b_ref.shape[-1] // 2
     rows = []
     for c in range(block):
-        parts = [x_ref[p, :, part, c].reshape(devices * slots, points).T
-                 for p in range(CHUNKS) for part in range(2)]
+        parts = [x_ref[:, part, c].reshape(devices * slots, points).T for part in range(2)]
         rows.append(jnp.concatenate(parts, axis=1))
     value = mm3(split(jnp.concatenate(rows, axis=0)), (b_ref[0], b_ref[1]))
+    return [value[:, part * freqs:(part + 1) * freqs].reshape(block, points, freqs) for part in range(2)]
+
+
+def finish_kernel(x_ref, b_ref, half_ref, o_ref):
+    value = to_frequency(x_ref, b_ref)
     for part in range(2):
-        o_ref[part] = value[:, part * freqs:(part + 1) * freqs].reshape(block, points, freqs)
+        o_ref[part] = half_ref[part] + value[part]
 
 
 def local(devices, green, pair_table, mirror_map):
@@ -262,19 +278,20 @@
     times = [owned_times(devices, freqs, p) for p in range(CHUNKS)]
     time_table = np.stack([np.stack(time_tables(t, freqs)) for t in times])
     plane_tables = np.stack(plane_table(side, 1.0) + plane_table(side, -1.0))
-    back = [frequency_tables(t, freqs) for t in times]
-    frequency_table = np.stack([np.concatenate([b[i] for b in back], axis=0) for i in range(2)])
+    frequency_table = [np.stack(frequency_tables(t, freqs)) for t in times]
     hbm = pl.BlockSpec(memory_space=pl.ANY)
     cells = (side, entries, slots, 2 * plane)
-    arrived = pl.pallas_call(
+    exchanged = (devices, 2, comps, slots, points)
+    result = (2, comps, points, freqs)
+    half, last = pl.pallas_call(
         main_kernel,
-        out_shape=jax.ShapeDtypeStruct((CHUNKS, devices, 2, comps, slots, points), f32),
-        in_specs=[SMEM, SMEM, hbm, hbm, hbm],
-        out_specs=hbm,
+        out_shape=[jax.ShapeDtypeStruct(result, f32), jax.ShapeDtypeStruct(exchanged, f32)],
+        in_specs=[SMEM, SMEM, pl.BlockSpec(memory_space=pltpu.VMEM), hbm, hbm, hbm],
+        out_specs=[hbm, hbm],
         scratch_shapes=[
-            pltpu.VMEM(green.shape, f32),
             pltpu.VMEM(time_table.shape, bf16),
             pltpu.VMEM(plane_tables.shape, bf16),
+            pltpu.VMEM(frequency_table[0].shape, bf16),
             pltpu.VMEM((2, 2 * plane, 2 * plane), bf16),
             pltpu.VMEM((CHUNKS, devices, 2, entries, slots, points), f32),
             pltpu.VMEM((CHUNKS, devices, 2, entries, slots, points), f32),
@@ -282,30 +299,34 @@
             pltpu.VMEM(cells, f32),
             pltpu.VMEM(cells, f32),
             pltpu.VMEM((comps,) + (side, slots, 2 * plane), f32),
-            pltpu.VMEM((CHUNKS, devices, 2, comps, slots, points), f32),
-            pltpu.SemaphoreType.DMA((3,)),
+            pltpu.VMEM((CHUNKS,) + exchanged, f32),
+            pltpu.VMEM(exchanged, f32),
+            pltpu.VMEM(result, f32),
+            pltpu.SemaphoreType.DMA((4,)),
             pltpu.SemaphoreType.DMA((2 * CHUNKS,)),
             pltpu.SemaphoreType.DMA((2 * CHUNKS,)),
             pltpu.SemaphoreType.DMA((2 * CHUNKS,)),
         ],
         compiler_params=pltpu.CompilerParams(
-            vmem_limit_bytes=56 * 1024 * 1024, collective_id=0, has_side_effects=True
+            vmem_limit_bytes=48 * 1024 * 1024, collective_id=0, has_side_effects=True
         ),
         cost_estimate=pl.CostEstimate(flops=18 * 10**9, bytes_accessed=16 * 2**20, transcendentals=0),
-    )(pair_table, mirror_map, green, time_table, plane_tables)
-    block = comps // 2
+    )(pair_table.T, mirror_map, green, time_table, plane_tables, frequency_table[0])
+    block = comps // 4
+    whole = pl.BlockSpec((2, block, points, freqs), lambda i: (0, i, 0, 0))
     return pl.pallas_call(
-        to_frequency_kernel,
+        finish_kernel,
         grid=(comps // block,),
-        out_shape=jax.ShapeDtypeStruct((2, comps, points, freqs), f32),
+        out_shape=jax.ShapeDtypeStruct(result, f32),
         in_specs=[
-            pl.BlockSpec((CHUNKS, devices, 2, block, slots, points), lambda i: (0, 0, 0, i, 0, 0)),
-            pl.BlockSpec((2, 2 * freqs, 2 * freqs), lambda i: (0, 0, 0)),
+            pl.BlockSpec((devices, 2, block, slots, points), lambda i: (0, 0, i, 0, 0)),
+            pl.BlockSpec(frequency_table[1].shape, lambda i: (0, 0, 0)),
+            whole,
         ],
-        out_specs=pl.BlockSpec((2, block, points, freqs), lambda i: (0, i, 0, 0)),
-        compiler_params=PARAMS,
-        cost_estimate=pl.CostEstimate(flops=12 * 10**9, bytes_accessed=16 * 2**20, transcendentals=0),
-    )(arrived, frequency_table)
+        out_specs=whole,
+        compiler_params=pltpu.CompilerParams(vmem_limit_bytes=58 * 1024 * 1024),
+        cost_estimate=pl.CostEstimate(flops=6 * 10**9, bytes_accessed=16 * 2**20, transcendentals=0),
+    )(last, frequency_table[1], half)
 
 
 def solution(mesh):

time: 160 us -> 158 us (0.988)
  Pallas kernels: 155 us -> 152 us
    pallas_call x2, Pallas kernels: 155 us -> 152 us  [the longest x1 144 us: local(): pl.pallas_call(main_kernel, out_shape=[jax.ShapeDtypeStruct(result, f32),...]
    unnamed x3 -> x8, local copies, waits for them, and re-layouts: 3.53 us -> 4.27 us
where the time goes in v2:
time: 158 us; the launch traced here: 156 us
  Pallas kernels  152 us (96%)
  local copies, waits for them, and re-layouts  4.27 us (3%)
    pallas_call x1, Pallas kernels, local(): pl.pallas_call(main_kernel, out_shape=[jax.ShapeDtypeStruct(result, f32),...  144 us
    pallas_call x1, Pallas kernels, local(): pl.pallas_call(finish_kernel, grid=(comps // block,), out_shape=jax.Shape...  8.08 us
    unnamed x8, local copies, waits for them, and re-layouts  4.27 us

profile of v2, /device:TPU:0, one launch (start us, length us, event | category | flops | bytes accessed | tf_op | source)
XLA Modules:
  0.0 156.4 jit_solution(2597105781517206861)
XLA Ops:
  0.0 0.0 copy-start
  0.0 1.6 %copy-done = f32[2,4,128,512]{3,2,1,0:T(8,128)S(1)} copy-done((f32[2,4,128,512]{3,2,1,0:T(8,128)S(1)}, f32[2,4,128,512]{3,2,1,0:T(8,128)}, u32[]{:S(2)}) %copy-start) | copy-done | bytes 2097176
  1.6 0.0 copy-start.1
  1.6 0.7 copy-done.1
  2.3 0.0 copy-start.2
  2.3 0.7 copy-done.2
  3.0 144.0 %shard_map.73 = (f32[2,8,128,512]{3,2,1,0:T(8,128)}, f32[32,2,8,8,128]{4,3,2,1,0:T(8,128)S(1)}) custom-call(s32[2,8]{1,0:T(2,128)S(1)} %bitcast.1, s32[3,16]{1,0:T(4,128)S(1)} %copy-done.1, f32[2,4,128,512]{3,2,1,0:T(8,128)S(1)} %copy-done, bf16[2,4,256,512]{3,2,1,0:T(8,128)(2,1)} %constant.8.clone.time_hbm, bf16[4,512,512]{2,1,0:T(8,128)(2,1)} %constant.9.clone.plane_hbm, ...), custom_call_target="tpu_custom_call" | custom-call | flops 17999998976 | bytes 16777216 | tf_op jit(solution)/shard_map/pallas_call | solution.py:286
  147.0 0.0 copy-start.3
  147.0 1.3 copy-done.3
  148.3 8.1 %shard_map.74 = f32[2,8,128,512]{3,2,1,0:T(8,128)} custom-call(f32[32,2,8,8,128]{4,3,2,1,0:T(8,128)} %copy-done.3, bf16[2,512,1024]{2,1,0:T(8,128)(2,1)} %constant.11.clone.b_ref, f32[2,8,128,512]{3,2,1,0:T(8,128)} %get-tuple-element.8.half_ref), custom_call_target="tpu_custom_call" | custom-call | flops 6000000000 | bytes 16777216 | tf_op jit(solution)/shard_map/pallas_call | solution.py:317
Async XLA Ops:
  0.0 1.6 %copy-start = (f32[2,4,128,512]{3,2,1,0:T(8,128)S(1)}, f32[2,4,128,512]{3,2,1,0:T(8,128)}, u32[]{:S(2)}) copy-start(f32[2,4,128,512]{3,2,1,0:T(8,128)} %green.1) | copy-start | bytes 6291460
  1.6 0.7 copy-start.1
  2.3 0.7 copy-start.2
  147.0 1.3 copy-start.3

commit v3 on v2

--- a/solution.py
+++ b/solution.py
@@ -165,17 +165,18 @@
     lax.fori_loop(0, comps, back, 0)
 
 
-def main_kernel(pair_ref, mirror_ref, green, time_hbm, plane_hbm, back_hbm, half_hbm, last,
-                table, planes, back, mirrored, tau, x, y, g, gm, chi, sent, got, acc,
+def main_kernel(pair_ref, mirror_ref, green_hbm, time_hbm, plane_hbm, back_hbm, half_hbm, last,
+                green, table, planes, back, mirrored, tau, x, y, g, gm, chi, sent, got, acc,
                 load, own, send, recv):
     devices = tau.shape[1]
     side = y.shape[0]
     plane = side * side
     me = lax.axis_index("kb")
     loads = [pltpu.make_async_copy(src, dst, load.at[i])
-             for i, (src, dst) in enumerate([(time_hbm, table), (plane_hbm, planes), (back_hbm, back)])]
-    for copy in loads:
-        copy.start()
+             for i, (src, dst) in enumerate([(time_hbm, table), (plane_hbm, planes), (back_hbm, back),
+                                       (green_hbm, green)])]
+    for i in (3, 0, 1, 2):
+        loads[i].start()
     barrier = pltpu.get_barrier_semaphore()
 
     def greet(s, carry):
@@ -210,6 +211,7 @@
         part = ref.at[pl.ds(0, devices - 1)]
         pltpu.make_async_copy(part, part, sem).wait()
 
+    loads[3].wait()
     loads[0].wait()
     for p in range(CHUNKS):
         to_time(green, table, tau, p)
@@ -241,7 +243,7 @@
         value = to_frequency(got.at[:, :, chosen], back)
         for part in range(2):
             acc[part, chosen] = value[part]
-    store = pltpu.make_async_copy(acc, half_hbm, load.at[3])
+    store = pltpu.make_async_copy(acc, half_hbm, load.at[4])
     store.start()
     for p in range(CHUNKS):
         finish(tau.at[p], send.at[p])
@@ -286,9 +288,10 @@
     half, last = pl.pallas_call(
         main_kernel,
         out_shape=[jax.ShapeDtypeStruct(result, f32), jax.ShapeDtypeStruct(exchanged, f32)],
-        in_specs=[SMEM, SMEM, pl.BlockSpec(memory_space=pltpu.VMEM), hbm, hbm, hbm],
+        in_specs=[SMEM, SMEM, hbm, hbm, hbm, hbm],
         out_specs=[hbm, hbm],
         scratch_shapes=[
+            pltpu.VMEM(green.shape, f32),
             pltpu.VMEM(time_table.shape, bf16),
             pltpu.VMEM(plane_tables.shape, bf16),
             pltpu.VMEM(frequency_table[0].shape, bf16),
@@ -302,13 +305,13 @@
             pltpu.VMEM((CHUNKS,) + exchanged, f32),
             pltpu.VMEM(exchanged, f32),
             pltpu.VMEM(result, f32),
-            pltpu.SemaphoreType.DMA((4,)),
+            pltpu.SemaphoreType.DMA((5,)),
             pltpu.SemaphoreType.DMA((2 * CHUNKS,)),
             pltpu.SemaphoreType.DMA((2 * CHUNKS,)),
             pltpu.SemaphoreType.DMA((2 * CHUNKS,)),
         ],
         compiler_params=pltpu.CompilerParams(
-            vmem_limit_bytes=48 * 1024 * 1024, collective_id=0, has_side_effects=True
+            vmem_limit_bytes=60 * 1024 * 1024, collective_id=0, has_side_effects=True
         ),
         cost_estimate=pl.CostEstimate(flops=18 * 10**9, bytes_accessed=16 * 2**20, transcendentals=0),
     )(pair_table.T, mirror_map, green, time_table, plane_tables, frequency_table[0])

time: 158 us -> 154 us (0.975)
  local copies, waits for them, and re-layouts: 4.27 us -> 0 us
    unnamed x8 -> x0, local copies, waits for them, and re-layouts: 4.27 us -> none
where the time goes in v3:
time: 154 us; the launch traced here: 153 us
  Pallas kernels  153 us (99%)
    pallas_call x1, Pallas kernels, local(): pl.pallas_call(main_kernel, out_shape=[jax.ShapeDtypeStruct(result, f32),...  145 us
    pallas_call x1, Pallas kernels, local(): pl.pallas_call(finish_kernel, grid=(comps // block,), out_shape=jax.Shape...  8.11 us

profile of v3, /device:TPU:0, one launch (start us, length us, event | category | flops | bytes accessed | tf_op | source)
XLA Modules:
  0.0 152.7 jit_solution(9875759316672152520)
XLA Ops:
  0.0 144.6 %shard_map.73 = (f32[2,8,128,512]{3,2,1,0:T(8,128)}, f32[32,2,8,8,128]{4,3,2,1,0:T(8,128)}) custom-call(s32[2,8]{1,0:T(2,128)} %bitcast.1, s32[3,16]{1,0:T(4,128)} %mirror_ref.1, f32[2,4,128,512]{3,2,1,0:T(8,128)} %green_hbm.1, bf16[2,4,256,512]{3,2,1,0:T(8,128)(2,1)} %constant.8.clone.time_hbm, bf16[4,512,512]{2,1,0:T(8,128)(2,1)} %constant.9.clone.plane_hbm, ...), custom_call_target="tpu_custom_call" | custom-call | flops 17999998976 | bytes 16777216 | tf_op jit(solution)/shard_map/pallas_call | solution.py:288
  144.6 8.1 %shard_map.74 = f32[2,8,128,512]{3,2,1,0:T(8,128)} custom-call(f32[32,2,8,8,128]{4,3,2,1,0:T(8,128)} %get-tuple-element.7.x_ref, bf16[2,512,1024]{2,1,0:T(8,128)(2,1)} %constant.11.clone.b_ref, f32[2,8,128,512]{3,2,1,0:T(8,128)} %get-tuple-element.8.half_ref), custom_call_target="tpu_custom_call" | custom-call | flops 6000000000 | bytes 16777216 | tf_op jit(solution)/shard_map/pallas_call | solution.py:320
